TPU v7x, 256 devices: a whole 4x4x8 slice. The times are simulated.
256 devices in a mesh: tok: 16 (over y_lo, z), voc: 16 (over y_hi, x, core).
Axes of the slice: x: 4, y: 4 (y_hi: 2, y_lo: 2; y = y_hi * 2 + y_lo), z: 8, core: 2. Of those that a mesh axis runs over, the one named last changes fastest.
Arguments:
- hidden: bfloat16 [1024, 8192], P('tok', 'voc'), may hold values from -200 to 200
- gain: float32 [8192], replicated, may hold values from 0.5 to 1.5
- head_weight: bfloat16 [8192, 131072], P(None, ('tok', 'voc')), may hold values from -10 to 10
- student: bfloat16 [1024, 131072], P(None, ('tok', 'voc')), may hold values from -30 to -2
- token_ids: int32 [1024], replicated, may hold values from 0 to 131071
- lengths: int32 [16], replicated, may hold values from 1 to 64
Outputs:
- divergence: float32 [1024], P('tok')
- token_logprob: float32 [1024], P('tok')
All inputs are finite; a program needn't handle non-finite values.
Results may differ from a plain program's by a relative error of at most 0.0023.
Values may be sent and summed in bfloat16 or wider, within the bound.
A program may use at most 128 MiB of HBM per device.

v0:
```python
import functools

import jax
import jax.numpy as jnp
from jax import lax
from jax.experimental import pallas as pl
from jax.experimental.pallas import tpu as pltpu
from jax.sharding import PartitionSpec as P

D = 8192
LEN = 64
EPS = 1e-06
MESH = pl.DeviceIdType.MESH
F32 = jnp.float32
BF16 = jnp.bfloat16
RING = {"y": 4, "x": 4, "z": 8}
NMSG = 44
VALL = slice(None)


def split3(value):
    hi = value.astype(BF16).astype(F32)
    rest = value - hi
    mid = rest.astype(BF16).astype(F32)
    return hi, mid, (rest - mid).astype(BF16).astype(F32)


def blocks_of(groups):
    blocks = [[] for _ in groups]
    start = 0
    for part, count in enumerate(groups):
        for _ in range(count // 2):
            blocks[part].append((start, 128))
            start += 128
    for part, count in enumerate(groups):
        if count % 2:
            blocks[part].append((start, 64))
            start += 64
    return blocks


def kernel(groups, hidden, gain, lens, ids, student, head, out, *scratch):
    cap = (sum(groups) + 1) // 2 * 128
    blocks = blocks_of(groups)
    lasts = ("x", "y", "z")
    slabs = scratch[:3]
    (w_all, st_all, h_in, gain_in, ids_in, onehot, st_rows, id_cols, acc, stats, gcol, r_rows, sq_buf, r_buf, a2a_out,
     a2a_in, fin_out, fin_a, fin_b, local_sem, pair_sem, send_sem, recv_sem) = scratch[3:]
    tok = lax.axis_index("tok")
    voc = lax.axis_index("voc")
    here = {"y": (voc // 8) * 2 + tok // 8, "x": (voc // 2) % 4, "z": tok % 8}
    core = voc % 2
    way = 1 - 2 * core

    def device(place, which):
        return {"tok": (place["y"] % 2) * 8 + place["z"], "voc": ((place["y"] // 2) * 4 + place["x"]) * 2 + which}

    def moved(axis, by):
        place = dict(here)
        place[axis] = lax.rem(here[axis] + by + RING[axis], RING[axis])
        return place

    def tok_peer(step):
        return {"tok": lax.rem(tok + step, 16), "voc": voc}

    def voc_peer(step):
        return {"tok": tok, "voc": lax.rem(voc + step, 16)}

    def plane_peer(step):
        return device({"y": lax.rem(here["y"] + step // 4, 4), "x": lax.rem(here["x"] + step % 4, 4), "z": here["z"]}, core)

    hidden_copy = pltpu.make_async_copy(hidden, h_in, local_sem.at[0])
    hidden_copy.start()
    barrier = pltpu.get_barrier_semaphore()

    def greet(step, carry):
        pl.semaphore_signal(barrier, inc=1, device_id=tok_peer(step), device_id_type=MESH)
        pl.semaphore_signal(barrier, inc=1, device_id=voc_peer(step), device_id_type=MESH)
        return carry

    lax.fori_loop(1, 16, greet, 0)
    for step in range(4, 16):
        dy, dx = step // 4, step % 4
        if dy % 2 and dx:
            pl.semaphore_signal(barrier, inc=1, device_id=plane_peer(step), device_id_type=MESH)
    across = {"tok": lax.rem(tok + 8, 16), "voc": lax.rem(voc + 8, 16)}
    pl.semaphore_signal(barrier, inc=1, device_id=across, device_id_type=MESH)

    def head_copy(index):
        y = (index // 16) * 2 + index % 2
        return pltpu.make_async_copy(
            head.at[index], w_all.at[(index // 2) % 2, y, (index // 4) % 4], local_sem.at[4]
        )

    gain_copy = pltpu.make_async_copy(gain, gain_in, local_sem.at[1])
    ids_copy = pltpu.make_async_copy(ids, ids_in, local_sem.at[2])
    student_copy = pltpu.make_async_copy(student, st_all, local_sem.at[3])
    hidden_copy.wait()
    rows = h_in[...].astype(F32)
    rows = jnp.concatenate([rows, rows], axis=0)
    turned = rows.T
    square = jnp.sum(turned * turned, axis=0, keepdims=True)
    sq_buf[0] = square
    lane = lax.broadcasted_iota(jnp.int32, (1, 128), 1)
    turned = turned.reshape(16, 32, 128)
    a2a_out[...] = jnp.where(lane[None] < 64, turned[:, 0:16], turned[:, 16:32]).astype(BF16)

    pl.semaphore_wait(barrier, 37)

    def sq_copy(step):
        return pltpu.make_async_remote_copy(
            src_ref=sq_buf.at[0], dst_ref=sq_buf.at[step], send_sem=pair_sem.at[0],
            recv_sem=pair_sem.at[1], device_id=voc_peer(step), device_id_type=MESH)

    def a2a_copy(step):
        return pltpu.make_async_remote_copy(
            src_ref=a2a_out.at[lax.rem(tok + step, 16)], dst_ref=a2a_in.at[tok], send_sem=pair_sem.at[2],
            recv_sem=pair_sem.at[3], device_id=tok_peer(step), device_id_type=MESH)

    def r_copy(step):
        return pltpu.make_async_remote_copy(
            src_ref=r_buf.at[tok], dst_ref=r_buf.at[tok], send_sem=pair_sem.at[8],
            recv_sem=pair_sem.at[9], device_id=tok_peer(step), device_id_type=MESH)

    def fin_a_copy(step):
        return pltpu.make_async_remote_copy(
            src_ref=fin_out.at[lax.rem(tok + step, 16)], dst_ref=fin_a.at[step], send_sem=pair_sem.at[4],
            recv_sem=pair_sem.at[5], device_id=tok_peer(step), device_id_type=MESH)

    def fin_b_copy(step):
        return pltpu.make_async_remote_copy(
            src_ref=fin_b.at[0], dst_ref=fin_b.at[step], send_sem=pair_sem.at[6],
            recv_sem=pair_sem.at[7], device_id=voc_peer(step), device_id_type=MESH)

    def start_all(copy):
        def body(step, carry):
            copy(step).start()
            return carry
        lax.fori_loop(1, 16, body, 0)

    def group(ref, first, at):
        view = ref.at[pl.ds(first, 15)]
        return pltpu.make_async_remote_copy(
            src_ref=view, dst_ref=view, send_sem=pair_sem.at[at], recv_sem=pair_sem.at[at + 1],
            device_id=tok_peer(1), device_id_type=MESH)

    sq_group, a2a_group, r_group = group(sq_buf, 1, 0), group(a2a_in, 0, 2), group(r_buf, 0, 8)
    fin_a_group, fin_b_group = group(fin_a, 1, 4), group(fin_b, 1, 6)

    start_all(a2a_copy)
    start_all(sq_copy)
    a2a_in[tok] = a2a_out[tok]

    gain_copy.start()
    ids_copy.start()
    student_copy.start()

    def load(index, carry):
        head_copy(index).start()
        return carry

    lax.fori_loop(0, 32, load, 0)

    place_of = []
    offset = jnp.int32(0)
    for pair in range(8):
        first, second = lens[2 * pair], lens[2 * pair + 1]
        low = jnp.where(lane < first, offset + lane, -1)
        high = jnp.where(lane - 64 < second, offset + first + lane - 64, -1)
        place_of.append(jnp.where(lane < 64, low, high))
        offset = offset + first + second
    place_of = jnp.concatenate(place_of, axis=1)

    def fill(block, carry):
        start = pl.multiple_of(block * 64, 64)
        want = lax.broadcasted_iota(jnp.int32, (64, 1024), 0) + start
        onehot[pl.ds(start, 64), :] = jnp.where(want == place_of, 1.0, 0.0).astype(BF16)
        return carry

    lax.fori_loop(0, cap // 64, fill, 0)


    a2a_group.wait_recv()
    pieces = []
    for pair in range(8):
        low, high = a2a_in[2 * pair].astype(F32), a2a_in[2 * pair + 1].astype(F32)
        upper = jnp.where(lane < 64, low, pltpu.roll(high, 64, 1))
        under = jnp.where(lane < 64, pltpu.roll(low, 64, 1), high)
        pieces.append(jnp.concatenate([upper, under], axis=0))
    block = jnp.concatenate(pieces, axis=1).astype(BF16)
    packed = lax.dot_general(block, onehot[...], (((1,), (1,)), ((), ())), preferred_element_type=F32)

    numbers = {}

    def number_of(*key):
        return numbers.setdefault(key, len(numbers))

    def push(n, sent, key, src, target):
        pltpu.make_async_remote_copy(
            src_ref=src, dst_ref=src, send_sem=send_sem.at[3 * n + sent], recv_sem=recv_sem.at[number_of(n, *key)],
            device_id=target, device_id_type=MESH).start()

    def arrive(n, key, view):
        pltpu.make_async_remote_copy(
            src_ref=view, dst_ref=view, send_sem=send_sem.at[0], recv_sem=recv_sem.at[number_of(n, *key)],
            device_id=mate, device_id_type=MESH).wait_recv()

    mate = device(here, 1 - core)
    y, x, z = here["y"], here["x"], here["z"]
    own = [slab.at[core, y, x, z] for slab in slabs]
    for n in range(3):
        for at, (start, wide) in enumerate(blocks[n]):
            if wide == 128:
                slabs[n][core, y, x, z, 32 * at:32 * at + 32] = packed[:, start:start + 128].astype(BF16)
            else:
                base = start // 128 * 128
                both = packed[:, base:base + 128]
                flipped = pltpu.roll(both, 64, 1)
                if start == base:
                    half = jnp.where(lane < 64, both[0:16], flipped[16:32])
                else:
                    half = jnp.where(lane < 64, flipped[0:16], both[16:32])
                slabs[n][core, y, x, z, 32 * at:32 * at + 16] = half.astype(BF16)
        if n < 2:
            for by in (4, 3, 5, 2, 6, 1, 7):
                push(n, 0, ("first",), own[n], device(moved("z", by), core))
        else:
            for step in (10, 2, 8, 6, 9, 11, 14, 1, 3, 4, 12, 5, 7, 13, 15):
                push(n, 0, ("first",), own[n], plane_peer(step))
    firsts = [slabs[0].at[core, y, x, pl.ds(0, 7)], slabs[1].at[core, y, x, pl.ds(0, 7)],
              slabs[2].at[core, pl.ds(0, 3), 0, pl.ds(0, 5)]]
    sent_views = []
    for n in (0, 1):
        sent_views += [firsts[n], slabs[n].at[0], slabs[n].at[:, :, pl.ds(0, 3), pl.ds(0, 5)]]
    sent_views += [firsts[2], slabs[2].at[0, :, :, pl.ds(0, 7)], slabs[2].at[0]]

    sq_group.wait_recv()
    total_sq = sq_buf[0]
    for step in range(1, 16):
        total_sq = total_sq + sq_buf[step]
    r_buf[tok] = lax.rsqrt(total_sq / D + EPS)
    start_all(r_copy)

    gain_copy.wait()

    def spread_gain(row, carry):
        wide = jnp.broadcast_to(gain_in[pl.ds(row, 1), :], (128, 128)).T
        index = row // 2
        y = (index // 16) * 2 + index % 2
        start = pl.multiple_of((row % 2) * 4, 4)
        gcol[(index // 2) % 2, y, (index // 4) % 4, pl.ds(start, 4)] = wide.reshape(4, 32, 128)
        return carry

    lax.fori_loop(0, 64, spread_gain, 0)

    def zero(block, carry):
        acc[pl.ds(pl.multiple_of(block * 64, 64), 64), :] = jnp.zeros((64, 512), F32)
        return carry

    lax.fori_loop(0, cap // 64, zero, 0)

    def piece(n, which, c_at, b_at):
        if n == 0:
            return slabs[0].at[which, b_at, c_at]
        return slabs[1].at[which, c_at, b_at]

    def plane(n, which, c_at):
        if n == 0:
            return slabs[0].at[which, :, c_at]
        if n == 1:
            return slabs[1].at[which, c_at]
        return slabs[2].at[which, :, :, c_at]

    def zhalf(c_at, half):
        return slabs[2].at[core, pl.ds(2 * half, 2), :, c_at]

    second = ("y", "x")

    def two_lines(n):
        return slabs[0].at[core, pl.ds(0, 2), x] if n == 0 else slabs[1].at[core, y, pl.ds(0, 2)]

    def two_planes(n, which):
        if n == 0:
            return slabs[0].at[which, :, pl.ds(0, 2)]
        if n == 1:
            return slabs[1].at[which, pl.ds(0, 2)]
        return slabs[2].at[which, :, :, pl.ds(0, 2)]

    def both_ways(n, name, b_at):
        axis = lasts[n]
        for side in (1, -1):
            push(n, 1, (name,), piece(n, core, here[axis], b_at), device(moved(axis, side), core))

    def go_on(n, name, b_at):
        axis = lasts[n]
        arrive(n, (name,), two_lines(n))
        push(n, 2, (name, "on"), piece(n, core, moved(axis, -way)[axis], b_at), device(moved(axis, way), core))

    def term_of(n, which, pick):
        weight = gcol[(which, *pick)].reshape(-1, 128)
        depth = weight.shape[0]
        lefts = []
        for at, (start, wide) in enumerate(blocks[n]):
            base = start // 128 * 128
            factor = r_rows[0:1, base:base + 128]
            if wide == 128:
                left = slabs[n][(which, *pick, slice(32 * at, 32 * at + 32))].astype(F32).reshape(depth, 128)
            else:
                left = slabs[n][(which, *pick, slice(32 * at, 32 * at + 16))].astype(F32).reshape(depth // 32, 16, 128)
                left = jnp.concatenate([left, pltpu.roll(left, 64, 2)], axis=1).reshape(depth, 128)
                if start != base:
                    factor = pltpu.roll(factor, 64, 1)
            lefts.append((left * factor * weight).astype(BF16)[:, :wide])
        left = jnp.concatenate(lefts, axis=1) if len(lefts) > 1 else lefts[0]
        right = w_all[(which, *pick)].reshape(depth, 512)
        return lax.dot_general(left, right, (((0,), (0,)), ((), ())), preferred_element_type=F32)

    def multiply(n, which, *picks):
        term = term_of(n, which, picks[0])
        for pick in picks[1:]:
            term = term + term_of(n, which, pick)
        row = 0
        for start, wide in blocks[n]:
            acc[start:start + wide, :] += term[row:row + wide]
            row += wide

    def shift(axis, by):
        return lax.rem(here[axis] + by, RING[axis])

    def each(count, work):
        def body(index, carry):
            work(index)
            return carry
        lax.fori_loop(0, count, body, 0)

    def both_cores(index):
        return lax.rem(core + index, 2)

    def whole(n, which, by):
        at = shift(lasts[n], by)
        multiply(n, which, (VALL, at, VALL) if n == 0 else (at, VALL, VALL))

    def some(n, which, by, steps):
        at = shift(lasts[n], by)
        places = [shift(second[n], step) for step in steps]
        multiply(n, which, *[(place, at, VALL) if n == 0 else (at, place, VALL) for place in places])

    def planes(count, first):
        each(2 * count, lambda index: multiply(
            2, both_cores(index // count), (VALL, VALL, shift("z", first + index % count))))

    def to_mate(n, sent, key, refs):
        for ref in refs:
            push(n, sent, ("mate", *key), ref, mate)

    def from_mate(n, key, view):
        arrive(n, ("mate", *key), view)

    for n in (0, 1):
        arrive(n, ("first",), firsts[n])
        axis = second[n]
        for side in (1, -1):
            push(n, 2, ("line",), piece(n, core, here[lasts[n]], here[axis]), device(moved(axis, side), core))
    for n in (0, 1):
        both_ways(n, "own", here[second[n]])
    arrive(2, ("first",), firsts[2])
    for half in (0, 1):
        for side in (1, -1):
            push(2, 1, ("wave", 0, half), zhalf(z, half), device(moved("z", side), core))
    to_mate(2, 2, (0,), [plane(2, core, z)])

    r_group.wait_recv()
    factors = [jnp.where(lane < 64, r_buf[2 * pair], r_buf[2 * pair + 1]) for pair in range(8)]
    factors = jnp.concatenate(factors, axis=1)
    factors = jnp.broadcast_to(factors, (16, 1024))
    digit_row = lax.broadcasted_iota(jnp.int32, (16, 1024), 0)
    table = jnp.zeros((16, 1024), F32)
    for digit, value in enumerate(split3(factors)):
        table = jnp.where(digit_row == digit, value, table)
    table = lax.dot_general(table.astype(BF16), onehot[...], (((1,), (1,)), ((), ())), preferred_element_type=F32)
    r_rows[...] = jnp.broadcast_to(table[0:1] + table[1:2] + table[2:3], r_rows.shape)

    pltpu.make_async_copy(w_all, w_all, local_sem.at[4]).wait()

    def zstep(step):
        for half in (0, 1):
            arrive(2, ("wave", step, half), slabs[2].at[core, pl.ds(0, 2), :, pl.ds(0, 2)])
            for side in (1, -1):
                at = moved("z", -side * (step + 1))["z"]
                if step < 2:
                    push(2, 1, ("wave", step + 1, half), zhalf(at, half), device(moved("z", side), core))
            if step == 2:
                push(2, 1, ("wave", 3, half), zhalf(moved("z", -way * 3)["z"], half), device(moved("z", way), core))
        sides = (step + 1, -step - 1)
        to_mate(2, 2, (step + 1,), [plane(2, core, moved("z", by)["z"]) for by in sides])

    ids_copy.wait()
    local_id = ids_in[...] - (tok * 16 + voc) * 512
    local_id = jnp.where((local_id >= 0) & (local_id < 512), local_id, 512)
    digits = jnp.where(lax.broadcasted_iota(jnp.int32, (16, 1024), 0) == 0, local_id // 256, local_id % 256)
    digits = digits.astype(F32).astype(BF16)
    cols = lax.dot_general(onehot[...], digits, (((1,), (1,)), ((), ())), preferred_element_type=F32)
    id_cols[...] = cols[:, 0:1] * 256.0 + cols[:, 1:2]
    student_copy.wait()
    st_rows[...] = jnp.dot(onehot[...], st_all[...], preferred_element_type=F32).astype(BF16)

    for n in (0, 1):
        axis = second[n]
        arrive(n, ("line",), two_lines(n))
        push(n, 2, ("opposite",), piece(n, core, here[lasts[n]], moved(axis, -way)[axis]), device(moved(axis, way), core))
    for n in (0, 1):
        axis = second[n]
        both_ways(n, "left", moved(axis, -1)[axis])
        both_ways(n, "right", moved(axis, 1)[axis])
    zstep(0)
    for n in (0, 1):
        go_on(n, "own", here[second[n]])
    for n in (0, 1):
        axis = second[n]
        arrive(n, ("opposite",), piece(n, core, here[lasts[n]], 0))
        both_ways(n, "far", moved(axis, 2)[axis])
    for n in (0, 1):
        to_mate(n, 2, (0,), [plane(n, core, here[lasts[n]])])
    zstep(1)

    def opposite(n, name, by):
        axis = second[n]
        b_at = moved(axis, by)[axis]
        arrive(n, (name, "on"), piece(n, core, here[lasts[n]], 0))
        c_at = moved(lasts[n], 2)[lasts[n]]
        to_mate(n, 2, ("far",) if name == "far" else ("early",), [piece(n, core, c_at, b_at)])

    for n in (0, 1):
        from_mate(n, (0,), plane(n, 1 - core, here[lasts[n]]))
        each(2, lambda index: whole(n, both_cores(index), 0))
    for n in (0, 1):
        go_on(n, "left", moved(second[n], -1)[second[n]])
    for n in (0, 1):
        go_on(n, "right", moved(second[n], 1)[second[n]])
    for n in (0, 1):
        opposite(n, "own", 0)
    zstep(2)
    from_mate(2, (0,), plane(2, 1 - core, z))
    from_mate(2, (1,), two_planes(2, 1 - core))
    from_mate(2, (2,), two_planes(2, 1 - core))
    planes(5, 6)
    for n in (0, 1):
        go_on(n, "far", moved(second[n], 2)[second[n]])
    for n in (0, 1):
        to_mate(n, 1, (1,), [plane(n, core, moved(lasts[n], side)[lasts[n]]) for side in (1, -1)])
    each(2, lambda index: whole(0, core, 1 + 2 * index))
    for n in (0, 1):
        opposite(n, "left", -1)
    for n in (0, 1):
        opposite(n, "right", 1)
    each(2, lambda index: whole(1, core, 1 + 2 * index))
    for half in (0, 1):
        arrive(2, ("wave", 3, half), zhalf(z, 0))
    at = moved("z", 4)["z"]
    to_mate(2, 2, (4,), [plane(2, core, at)])
    from_mate(0, (1,), two_planes(0, 1 - core))
    each(2, lambda index: whole(0, 1 - core, 1 + 2 * index))
    for n in (0, 1):
        opposite(n, "far", 2)
    from_mate(1, (1,), two_planes(1, 1 - core))
    each(2, lambda index: whole(1, 1 - core, 1 + 2 * index))
    from_mate(2, (3,), two_planes(2, 1 - core))
    from_mate(2, (4,), plane(2, 1 - core, at))
    planes(3, 3)
    for n in (0, 1):
        three = slabs[0].at[core, pl.ds(0, 3), x] if n == 0 else slabs[1].at[core, y, pl.ds(0, 3)]
        from_mate(n, ("early",), three)
        from_mate(n, ("far",), piece(n, 1 - core, here[lasts[n]], 0))
        each(2, lambda index: whole(n, both_cores(index), 2))

    lanes128 = lax.broadcasted_iota(jnp.int32, (64, 128), 1)
    lanes512 = lax.broadcasted_iota(jnp.int32, (64, 512), 1).astype(F32)

    def partials(start):
        take = pl.ds(start, 64)
        logits = acc[take, :]
        top = jnp.max(logits, axis=1, keepdims=True)
        low = logits - top
        expo = jnp.exp(low)
        total = jnp.sum(expo, axis=1, keepdims=True)
        cross = jnp.sum(expo * (low - st_rows[take, :].astype(F32)), axis=1, keepdims=True)
        pick = jnp.sum(jnp.where(lanes512 == id_cols[take, :], logits, 0.0), axis=1, keepdims=True)
        table = jnp.zeros((64, 128), F32)
        for at, value in enumerate((top, total, cross, pick)):
            for digit, part in enumerate(split3(value)):
                table = jnp.where(lanes128 == 8 * digit + at, part, table)
        stats[take, :] = table.astype(BF16)

    assert len(numbers) == NMSG, len(numbers)
    def partials256(block, carry):
        for piece in range(4):
            partials(pl.multiple_of(block * 256 + piece * 64, 64))
        return carry

    lax.fori_loop(0, cap // 256, partials256, 0)
    if cap % 256:
        partials(cap - 128)
        partials(cap - 64)
    spread = lax.dot_general(stats[...], onehot[...], (((0,), (0,)), ((), ())), preferred_element_type=F32)
    spread = spread[0:8] + spread[8:16] + spread[16:24]
    for pair in range(8):
        rows4 = spread[:, 128 * pair:128 * (pair + 1)]
        turned4 = pltpu.roll(rows4, 64, 1)
        fin_out[2 * pair] = jnp.where(lane < 64, rows4[0:2], turned4[2:4])
        fin_out[2 * pair + 1] = jnp.where(lane < 64, turned4[0:2], rows4[2:4])
    start_all(fin_a_copy)
    fin_a[0] = fin_out[tok]
    for at, view in enumerate(sent_views):
        pltpu.make_async_remote_copy(
            src_ref=view, dst_ref=view, send_sem=send_sem.at[at], recv_sem=recv_sem.at[0], device_id=mate,
            device_id_type=MESH).wait_send()
    for copies in (sq_group, a2a_group, r_group):
        copies.wait_send()
    fin_a_group.wait_recv()

    def combine(ref):
        every = ref[...]
        top, total = every[:, 0:1, :], every[:, 1:2, :]
        cross, pick = pltpu.roll(top, 64, 2), pltpu.roll(total, 64, 2)
        most = jnp.max(top, axis=0, keepdims=True)
        gap = top - most
        scale = jnp.exp(gap)
        return (most[0], jnp.sum(scale * total, axis=0), jnp.sum(scale * (cross + gap * total), axis=0),
                jnp.sum(pick, axis=0))

    sub = lax.broadcasted_iota(jnp.int32, (8, 128), 0)

    def table_of(values):
        table = jnp.zeros((8, 128), F32)
        for at, value in enumerate(values):
            table = jnp.where(sub == at, value, table)
        return table

    top, total, cross, pick = combine(fin_a)
    fin_b[0] = jnp.concatenate(
        [jnp.where(lane < 64, top, pltpu.roll(cross, 64, 1)), jnp.where(lane < 64, total, pltpu.roll(pick, 64, 1))], axis=0)
    start_all(fin_b_copy)
    fin_b_group.wait_recv()
    top, total, cross, pick = combine(fin_b)
    log_total = jnp.log(total)
    kl = cross / total - log_total
    logprob = pick - (top + log_total)
    valid = lane < lens[tok]
    out[...] = table_of((jnp.where(valid, kl, 0.0), jnp.where(valid, logprob, 0.0)))
    fin_a_group.wait_send()
    fin_b_group.wait_send()


def run(groups, number, hidden, gain, lengths, ids, student, head):
    cap = (sum(groups) + 1) // 2 * 128
    hbm = pl.BlockSpec(memory_space=pl.ANY)
    return pl.pallas_call(
        functools.partial(kernel, groups),
        out_shape=jax.ShapeDtypeStruct((8, 128), F32),
        in_specs=[hbm, hbm, pl.BlockSpec(memory_space=pltpu.SMEM), hbm, hbm, hbm],
        out_specs=pl.BlockSpec(memory_space=pltpu.VMEM),
        scratch_shapes=[pltpu.VMEM((2, 4, 4, 8, 16 * count, 128), BF16) for count in groups] + [
            pltpu.VMEM((2, 4, 4, 8, 32, 512), BF16),
            pltpu.VMEM((1024, 512), BF16),
            pltpu.VMEM((64, 512), BF16),
            pltpu.VMEM((64, 128), F32),
            pltpu.VMEM((1, 1024), jnp.int32),
            pltpu.VMEM((cap, 1024), BF16),
            pltpu.VMEM((cap, 512), BF16),
            pltpu.VMEM((cap, 1), F32),
            pltpu.VMEM((cap, 512), F32),
            pltpu.VMEM((cap, 128), BF16),
            pltpu.VMEM((2, 4, 4, 8, 32, 128), F32),
            pltpu.VMEM((8, cap), F32),
            pltpu.VMEM((16, 1, 128), F32),
            pltpu.VMEM((16, 1, 128), F32),
            pltpu.VMEM((16, 16, 128), BF16),
            pltpu.VMEM((16, 16, 128), BF16),
            pltpu.VMEM((16, 2, 128), F32),
            pltpu.VMEM((16, 2, 128), F32),
            pltpu.VMEM((16, 2, 128), F32),
            pltpu.SemaphoreType.DMA((5,)),
            pltpu.SemaphoreType.DMA((10,)),
            pltpu.SemaphoreType.DMA((9,)),
            pltpu.SemaphoreType.DMA((NMSG,)),
        ],
        compiler_params=pltpu.CompilerParams(
            collective_id=number, has_side_effects=True, vmem_limit_bytes=60 * 1024 * 1024),
        name="gathered_head_%d" % (64 * sum(groups)),
    )(hidden, gain, lengths, ids, student, head)


SPLITS = ((3, 3, 2), (3, 3, 3), (4, 4, 2), (6, 6, 4))


def per_device(hidden, gain, head_weight, student, token_ids, lengths):
    args = (hidden, gain.reshape(64, 128), lengths, token_ids.reshape(1, -1), student,
            head_weight.reshape(32, 8, 32, head_weight.shape[1]))
    if len(SPLITS) == 1:
        table = run(SPLITS[0], 0, *args)
    else:
        tokens = jnp.sum(lengths)
        which = sum((tokens > 64 * sum(groups)).astype(jnp.int32) for groups in SPLITS[:-1])
        table = lax.switch(which, [functools.partial(run, groups, at) for at, groups in enumerate(SPLITS)], *args)
    return table[0, :64], table[1, :64]


def solution(mesh):
    placed = (P("tok", "voc"), P(), P(None, ("tok", "voc")), P(None, ("tok", "voc")), P(), P())
    return jax.shard_map(
        per_device, mesh=mesh, in_specs=placed, out_specs=(P("tok"), P("tok")), check_vma=False
    )
```

profile of v0, /device:TPU:1, one launch (start us, length us, event | category | flops | bytes accessed | tf_op | source)
XLA Modules:
  0.0 68.6 jit_solution(11555906978655197798)
XLA Ops:
  0.6 1.3 %reduce_sum.9 = s32[]{:T(128)} reduce(s32[16]{0:T(128)} %param.15, s32[]{:T(128)} %constant.0.clone.1), dimensions={0}, to_apply=%region_0.0 | reduce | flops 15 | bytes 72 | tf_op jit(solution)/shard_map/reduce_sum | solution.py:602
  3.9 64.2 %conditional.1 = (f32[8,128]{1,0:T(8,128)S(1)}) conditional(s32[]{:T(128)} %clamp.3, (bf16[64,512]{1,0:T(8,128)(2,1)}, f32[64,128]{1,0:T(8,128)}, s32[16]{0:T(128)}, s32[1,1024]{1,0:T(1,128)}, bf16[1024,512]{1,0:T(8,128)(2,1)}, /*index=5*/bf16[32,8,32,512]{3,2,1,0:T(8,128)(2,1)}) %tuple.35, ...), branch_computations={%region_1.0_spmd, %region_2.0_spmd, %region_3.0_spmd, %region_4.0_... | conditional | bytes 8 | solution.py:604
  3.9 63.5 %gathered_head_512.1 = f32[8,128]{1,0:T(8,128)S(1)} custom-call(bf16[64,512]{1,0:T(8,128)(2,1)} %get-tuple-element.28.hidden, f32[64,128]{1,0:T(8,128)} %get-tuple-element.29.gain, s32[16]{0:T(128)} %get-tuple-element.48.lens, s32[1,1024]{1,0:T(1,128)} %get-tuple-element.56.ids, bf16[1024,512]{1,0:T(8,128)(2,1)} %get-tuple-element.57.student, ...), custom_call_target="tpu_custom_call" | custom-call | tf_op jit(solution)/shard_map/cond/branch_0_fun/gathered_head_512/pallas_call | solution.py:557
  68.1 0.5 slice_bitcast_fusion
where the time goes:
time: 68.8 us; the launch traced here: 68.6 us
  Pallas kernels  63.5 us (92%)
  between operations  2.59 us (4%)
  other arithmetic  1.29 us (2%)
  loops' own time  0.73 us (1%)
    pallas_call x1, Pallas kernels, run(): pl.pallas_call(functools.partial(kernel, groups), out_shape=jax.ShapeDtyp...  63.5 us

commit v1 on v0

--- a/solution.py
+++ b/solution.py
@@ -14,7 +14,6 @@
 F32 = jnp.float32
 BF16 = jnp.bfloat16
 RING = {"y": 4, "x": 4, "z": 8}
-NMSG = 44
 VALL = slice(None)
 
 
@@ -30,12 +29,11 @@
     start = 0
     for part, count in enumerate(groups):
         for _ in range(count // 2):
-            blocks[part].append((start, 128))
+            blocks[part].append((start, 0, 32))
             start += 128
-    for part, count in enumerate(groups):
-        if count % 2:
-            blocks[part].append((start, 64))
-            start += 64
+    if groups[0] % 2:
+        blocks[0].append((start, 0, 16))
+        blocks[1].append((start, 16, 16))
     return blocks
 
 
@@ -43,6 +41,7 @@
     cap = (sum(groups) + 1) // 2 * 128
     blocks = blocks_of(groups)
     lasts = ("x", "y", "z")
+    has_z = groups[2] > 0
     slabs = scratch[:3]
     (w_all, st_all, h_in, gain_in, ids_in, onehot, st_rows, id_cols, acc, stats, gcol, r_rows, sq_buf, r_buf, a2a_out,
      a2a_in, fin_out, fin_a, fin_b, local_sem, pair_sem, send_sem, recv_sem) = scratch[3:]
@@ -81,7 +80,7 @@
     lax.fori_loop(1, 16, greet, 0)
     for step in range(4, 16):
         dy, dx = step // 4, step % 4
-        if dy % 2 and dx:
+        if dy % 2 and dx and has_z:
             pl.semaphore_signal(barrier, inc=1, device_id=plane_peer(step), device_id_type=MESH)
     across = {"tok": lax.rem(tok + 8, 16), "voc": lax.rem(voc + 8, 16)}
     pl.semaphore_signal(barrier, inc=1, device_id=across, device_id_type=MESH)
@@ -105,7 +104,7 @@
     turned = turned.reshape(16, 32, 128)
     a2a_out[...] = jnp.where(lane[None] < 64, turned[:, 0:16], turned[:, 16:32]).astype(BF16)
 
-    pl.semaphore_wait(barrier, 37)
+    pl.semaphore_wait(barrier, 37 if has_z else 31)
 
     def sq_copy(step):
         return pltpu.make_async_remote_copy(
@@ -180,6 +179,17 @@
     lax.fori_loop(0, cap // 64, fill, 0)
 
 
+    gain_copy.wait()
+
+    def spread_gain(row, carry):
+        wide = jnp.broadcast_to(gain_in[pl.ds(row, 1), :], (128, 128)).T
+        index = row // 2
+        y = (index // 16) * 2 + index % 2
+        start = pl.multiple_of((row % 2) * 4, 4)
+        gcol[(index // 2) % 2, y, (index // 4) % 4, pl.ds(start, 4)] = wide.reshape(4, 32, 128)
+        return carry
+
+    lax.fori_loop(0, 32, spread_gain, 0, unroll=2)
     a2a_group.wait_recv()
     pieces = []
     for pair in range(8):
@@ -196,11 +206,15 @@
         return numbers.setdefault(key, len(numbers))
 
     def push(n, sent, key, src, target):
+        if n == 2 and not has_z:
+            return
         pltpu.make_async_remote_copy(
             src_ref=src, dst_ref=src, send_sem=send_sem.at[3 * n + sent], recv_sem=recv_sem.at[number_of(n, *key)],
             device_id=target, device_id_type=MESH).start()
 
     def arrive(n, key, view):
+        if n == 2 and not has_z:
+            return
         pltpu.make_async_remote_copy(
             src_ref=view, dst_ref=view, send_sem=send_sem.at[0], recv_sem=recv_sem.at[number_of(n, *key)],
             device_id=mate, device_id_type=MESH).wait_recv()
@@ -209,22 +223,12 @@
     y, x, z = here["y"], here["x"], here["z"]
     own = [slab.at[core, y, x, z] for slab in slabs]
     for n in range(3):
-        for at, (start, wide) in enumerate(blocks[n]):
-            if wide == 128:
-                slabs[n][core, y, x, z, 32 * at:32 * at + 32] = packed[:, start:start + 128].astype(BF16)
-            else:
-                base = start // 128 * 128
-                both = packed[:, base:base + 128]
-                flipped = pltpu.roll(both, 64, 1)
-                if start == base:
-                    half = jnp.where(lane < 64, both[0:16], flipped[16:32])
-                else:
-                    half = jnp.where(lane < 64, flipped[0:16], both[16:32])
-                slabs[n][core, y, x, z, 32 * at:32 * at + 16] = half.astype(BF16)
+        for at, (start, row, rows) in enumerate(blocks[n]):
+            slabs[n][core, y, x, z, 32 * at:32 * at + rows] = packed[row:row + rows, start:start + 128].astype(BF16)
         if n < 2:
             for by in (4, 3, 5, 2, 6, 1, 7):
                 push(n, 0, ("first",), own[n], device(moved("z", by), core))
-        else:
+        elif has_z:
             for step in (10, 2, 8, 6, 9, 11, 14, 1, 3, 4, 12, 5, 7, 13, 15):
                 push(n, 0, ("first",), own[n], plane_peer(step))
     firsts = [slabs[0].at[core, y, x, pl.ds(0, 7)], slabs[1].at[core, y, x, pl.ds(0, 7)],
@@ -232,7 +236,8 @@
     sent_views = []
     for n in (0, 1):
         sent_views += [firsts[n], slabs[n].at[0], slabs[n].at[:, :, pl.ds(0, 3), pl.ds(0, 5)]]
-    sent_views += [firsts[2], slabs[2].at[0, :, :, pl.ds(0, 7)], slabs[2].at[0]]
+    if has_z:
+        sent_views += [firsts[2], slabs[2].at[0, :, :, pl.ds(0, 7)], slabs[2].at[0]]
 
     sq_group.wait_recv()
     total_sq = sq_buf[0]
@@ -241,17 +246,7 @@
     r_buf[tok] = lax.rsqrt(total_sq / D + EPS)
     start_all(r_copy)
 
-    gain_copy.wait()
-
-    def spread_gain(row, carry):
-        wide = jnp.broadcast_to(gain_in[pl.ds(row, 1), :], (128, 128)).T
-        index = row // 2
-        y = (index // 16) * 2 + index % 2
-        start = pl.multiple_of((row % 2) * 4, 4)
-        gcol[(index // 2) % 2, y, (index // 4) % 4, pl.ds(start, 4)] = wide.reshape(4, 32, 128)
-        return carry
-
-    lax.fori_loop(0, 64, spread_gain, 0)
+    lax.fori_loop(32, 64, spread_gain, 0, unroll=2)
 
     def zero(block, carry):
         acc[pl.ds(pl.multiple_of(block * 64, 64), 64), :] = jnp.zeros((64, 512), F32)
@@ -296,38 +291,32 @@
         arrive(n, (name,), two_lines(n))
         push(n, 2, (name, "on"), piece(n, core, moved(axis, -way)[axis], b_at), device(moved(axis, way), core))
 
-    def term_of(n, which, pick):
-        weight = gcol[(which, *pick)].reshape(-1, 128)
-        depth = weight.shape[0]
-        lefts = []
-        for at, (start, wide) in enumerate(blocks[n]):
-            base = start // 128 * 128
-            factor = r_rows[0:1, base:base + 128]
-            if wide == 128:
-                left = slabs[n][(which, *pick, slice(32 * at, 32 * at + 32))].astype(F32).reshape(depth, 128)
-            else:
-                left = slabs[n][(which, *pick, slice(32 * at, 32 * at + 16))].astype(F32).reshape(depth // 32, 16, 128)
-                left = jnp.concatenate([left, pltpu.roll(left, 64, 2)], axis=1).reshape(depth, 128)
-                if start != base:
-                    factor = pltpu.roll(factor, 64, 1)
-            lefts.append((left * factor * weight).astype(BF16)[:, :wide])
-        left = jnp.concatenate(lefts, axis=1) if len(lefts) > 1 else lefts[0]
-        right = w_all[(which, *pick)].reshape(depth, 512)
-        return lax.dot_general(left, right, (((0,), (0,)), ((), ())), preferred_element_type=F32)
-
-    def multiply(n, which, *picks):
-        term = term_of(n, which, picks[0])
-        for pick in picks[1:]:
-            term = term + term_of(n, which, pick)
-        row = 0
-        for start, wide in blocks[n]:
-            acc[start:start + wide, :] += term[row:row + wide]
-            row += wide
+    def multiply(n, which, pick):
+        if n == 2 and not has_z:
+            return
+        for row, rows in ((0, 32), (0, 16), (16, 16)):
+            chosen = [(at, block[0]) for at, block in enumerate(blocks[n]) if block[1:] == (row, rows)]
+            if not chosen:
+                continue
+            take = (which, *pick, slice(row, row + rows))
+            weight = gcol[take].reshape(-1, 128)
+            depth = weight.shape[0]
+            lefts = []
+            for at, start in chosen:
+                left = slabs[n][(which, *pick, slice(32 * at, 32 * at + rows))].astype(F32).reshape(depth, 128)
+                lefts.append((left * r_rows[0:1, start:start + 128] * weight).astype(BF16))
+            left = jnp.concatenate(lefts, axis=1) if len(lefts) > 1 else lefts[0]
+            right = w_all[take].reshape(depth, 512)
+            term = lax.dot_general(left, right, (((0,), (0,)), ((), ())), preferred_element_type=F32)
+            first = chosen[0][1]
+            acc[first:first + 128 * len(chosen), :] += term
 
     def shift(axis, by):
         return lax.rem(here[axis] + by, RING[axis])
 
-    def each(count, work):
+    def each(count, work, wanted=True):
+        if not wanted:
+            return
         def body(index, carry):
             work(index)
             return carry
@@ -340,14 +329,8 @@
         at = shift(lasts[n], by)
         multiply(n, which, (VALL, at, VALL) if n == 0 else (at, VALL, VALL))
 
-    def some(n, which, by, steps):
-        at = shift(lasts[n], by)
-        places = [shift(second[n], step) for step in steps]
-        multiply(n, which, *[(place, at, VALL) if n == 0 else (at, place, VALL) for place in places])
-
-    def planes(count, first):
-        each(2 * count, lambda index: multiply(
-            2, both_cores(index // count), (VALL, VALL, shift("z", first + index % count))))
+    def planes(which, count, first, stride=1):
+        each(count, lambda index: multiply(2, which, (VALL, VALL, shift("z", first + stride * index))), has_z)
 
     def to_mate(n, sent, key, refs):
         for ref in refs:
@@ -364,7 +347,7 @@
     for n in (0, 1):
         both_ways(n, "own", here[second[n]])
     arrive(2, ("first",), firsts[2])
-    for half in (0, 1):
+    for half in (0, 1) if has_z else ():
         for side in (1, -1):
             push(2, 1, ("wave", 0, half), zhalf(z, half), device(moved("z", side), core))
     to_mate(2, 2, (0,), [plane(2, core, z)])
@@ -413,6 +396,7 @@
         both_ways(n, "left", moved(axis, -1)[axis])
         both_ways(n, "right", moved(axis, 1)[axis])
     zstep(0)
+    planes(core, 3, 7)
     for n in (0, 1):
         go_on(n, "own", here[second[n]])
     for n in (0, 1):
@@ -421,6 +405,9 @@
         both_ways(n, "far", moved(axis, 2)[axis])
     for n in (0, 1):
         to_mate(n, 2, (0,), [plane(n, core, here[lasts[n]])])
+    from_mate(2, (0,), plane(2, 1 - core, z))
+    from_mate(2, (1,), two_planes(2, 1 - core))
+    planes(1 - core, 3, 7)
     zstep(1)
 
     def opposite(n, name, by):
@@ -439,16 +426,16 @@
         go_on(n, "right", moved(second[n], 1)[second[n]])
     for n in (0, 1):
         opposite(n, "own", 0)
+    planes(core, 2, 2, 4)
     zstep(2)
-    from_mate(2, (0,), plane(2, 1 - core, z))
-    from_mate(2, (1,), two_planes(2, 1 - core))
     from_mate(2, (2,), two_planes(2, 1 - core))
-    planes(5, 6)
+    planes(1 - core, 2, 2, 4)
     for n in (0, 1):
         go_on(n, "far", moved(second[n], 2)[second[n]])
     for n in (0, 1):
         to_mate(n, 1, (1,), [plane(n, core, moved(lasts[n], side)[lasts[n]]) for side in (1, -1)])
     each(2, lambda index: whole(0, core, 1 + 2 * index))
+    planes(core, 2, 3, 2)
     for n in (0, 1):
         opposite(n, "left", -1)
     for n in (0, 1):
@@ -465,8 +452,9 @@
     from_mate(1, (1,), two_planes(1, 1 - core))
     each(2, lambda index: whole(1, 1 - core, 1 + 2 * index))
     from_mate(2, (3,), two_planes(2, 1 - core))
+    planes(1 - core, 2, 3, 2)
     from_mate(2, (4,), plane(2, 1 - core, at))
-    planes(3, 3)
+    each(2, lambda index: multiply(2, both_cores(index), (VALL, VALL, shift("z", 4))), has_z)
     for n in (0, 1):
         three = slabs[0].at[core, pl.ds(0, 3), x] if n == 0 else slabs[1].at[core, y, pl.ds(0, 3)]
         from_mate(n, ("early",), three)
@@ -491,7 +479,7 @@
                 table = jnp.where(lanes128 == 8 * digit + at, part, table)
         stats[take, :] = table.astype(BF16)
 
-    assert len(numbers) == NMSG, len(numbers)
+    assert len(numbers) == (44 if has_z else 30)
     def partials256(block, carry):
         for piece in range(4):
             partials(pl.multiple_of(block * 256 + piece * 64, 64))
@@ -501,7 +489,7 @@
     if cap % 256:
         partials(cap - 128)
         partials(cap - 64)
-    spread = lax.dot_general(stats[...], onehot[...], (((0,), (0,)), ((), ())), preferred_element_type=F32)
+    spread = lax.dot_general(stats[...][:, 0:32], onehot[...], (((0,), (0,)), ((), ())), preferred_element_type=F32)
     spread = spread[0:8] + spread[8:16] + spread[16:24]
     for pair in range(8):
         rows4 = spread[:, 128 * pair:128 * (pair + 1)]
@@ -559,7 +547,7 @@
         out_shape=jax.ShapeDtypeStruct((8, 128), F32),
         in_specs=[hbm, hbm, pl.BlockSpec(memory_space=pltpu.SMEM), hbm, hbm, hbm],
         out_specs=pl.BlockSpec(memory_space=pltpu.VMEM),
-        scratch_shapes=[pltpu.VMEM((2, 4, 4, 8, 16 * count, 128), BF16) for count in groups] + [
+        scratch_shapes=[pltpu.VMEM((2, 4, 4, 8, 16 * max(count, 1), 128), BF16) for count in groups] + [
             pltpu.VMEM((2, 4, 4, 8, 32, 512), BF16),
             pltpu.VMEM((1024, 512), BF16),
             pltpu.VMEM((64, 512), BF16),
@@ -582,7 +570,7 @@
             pltpu.SemaphoreType.DMA((5,)),
             pltpu.SemaphoreType.DMA((10,)),
             pltpu.SemaphoreType.DMA((9,)),
-            pltpu.SemaphoreType.DMA((NMSG,)),
+            pltpu.SemaphoreType.DMA((44 if groups[2] else 30,)),
         ],
         compiler_params=pltpu.CompilerParams(
             collective_id=number, has_side_effects=True, vmem_limit_bytes=60 * 1024 * 1024),
@@ -590,7 +578,7 @@
     )(hidden, gain, lengths, ids, student, head)
 
 
-SPLITS = ((3, 3, 2), (3, 3, 3), (4, 4, 2), (6, 6, 4))
+SPLITS = ((3, 3, 2), (4, 4, 2), (6, 6, 4))
 
 
 def per_device(hidden, gain, head_weight, student, token_ids, lengths):

time: 68.8 us -> 63.3 us (0.920)
  Pallas kernels: 63.5 us -> 59.1 us
    pallas_call x1, Pallas kernels: 63.5 us -> 59.1 us  [run(): pl.pallas_call(functools.partial(kernel, groups), out_shape=jax.ShapeDtyp...]
where the time goes in v1:
time: 63.3 us; the launch traced here: 63.2 us
  Pallas kernels  59.1 us (93%)
  between operations  1.94 us (3%)
  other arithmetic  1.29 us (2%)
    pallas_call x1, Pallas kernels, run(): pl.pallas_call(functools.partial(kernel, groups), out_shape=jax.ShapeDtyp...  59.1 us
    reduce_sum x1, other arithmetic, per_device(): tokens = jnp.sum(lengths)  1.29 us

profile of v1, /device:TPU:1, one launch (start us, length us, event | category | flops | bytes accessed | tf_op | source)
XLA Modules:
  0.0 63.2 jit_solution(449847704254357669)
XLA Ops:
  0.6 1.3 %reduce_sum.9 = s32[]{:T(128)} reduce(s32[16]{0:T(128)} %param.14, s32[]{:T(128)} %constant.0.clone.1), dimensions={0}, to_apply=%region_0.0 | reduce | flops 15 | bytes 72 | tf_op jit(solution)/shard_map/reduce_sum | solution.py:590
  3.2 59.4 %conditional.1 = (f32[8,128]{1,0:T(8,128)S(1)}) conditional(s32[]{:T(128)} %clamp.3, (bf16[64,512]{1,0:T(8,128)(2,1)}, f32[64,128]{1,0:T(8,128)}, s32[16]{0:T(128)}, s32[1,1024]{1,0:T(1,128)}, bf16[1024,512]{1,0:T(8,128)(2,1)}, /*index=5*/bf16[32,8,32,512]{3,2,1,0:T(8,128)(2,1)}) %tuple.29, (bf16[64,512]{1,0:T(8,128)(2,1)}, ...), branch_computations={%region_1.0_spmd, %region_2.0_spmd, %region_3.0_spmd} | conditional | bytes 8 | solution.py:592
  3.2 59.1 %gathered_head_512.1 = f32[8,128]{1,0:T(8,128)S(1)} custom-call(bf16[64,512]{1,0:T(8,128)(2,1)} %get-tuple-element.28.hidden, f32[64,128]{1,0:T(8,128)} %get-tuple-element.29.gain, s32[16]{0:T(128)} %get-tuple-element.42.lens, s32[1,1024]{1,0:T(1,128)} %get-tuple-element.43.ids, bf16[1024,512]{1,0:T(8,128)(2,1)} %get-tuple-element.44.student, ...), custom_call_target="tpu_custom_call" | custom-call | tf_op jit(solution)/shard_map/cond/branch_0_fun/gathered_head_512/pallas_call | solution.py:545
  62.6 0.5 slice_bitcast_fusion

commit v2 on v1

--- a/solution.py
+++ b/solution.py
@@ -445,14 +445,14 @@
         arrive(2, ("wave", 3, half), zhalf(z, 0))
     at = moved("z", 4)["z"]
     to_mate(2, 2, (4,), [plane(2, core, at)])
+    from_mate(2, (3,), two_planes(2, 1 - core))
+    planes(1 - core, 2, 3, 2)
     from_mate(0, (1,), two_planes(0, 1 - core))
     each(2, lambda index: whole(0, 1 - core, 1 + 2 * index))
     for n in (0, 1):
         opposite(n, "far", 2)
     from_mate(1, (1,), two_planes(1, 1 - core))
     each(2, lambda index: whole(1, 1 - core, 1 + 2 * index))
-    from_mate(2, (3,), two_planes(2, 1 - core))
-    planes(1 - core, 2, 3, 2)
     from_mate(2, (4,), plane(2, 1 - core, at))
     each(2, lambda index: multiply(2, both_cores(index), (VALL, VALL, shift("z", 4))), has_z)
     for n in (0, 1):

time: 63.3 us -> 62.8 us (level)
  no operation moved by 1% of the time
where the time goes in v2:
time: 62.8 us; the launch traced here: 62.6 us
  Pallas kernels  58.6 us (93%)
  between operations  1.94 us (3%)
  other arithmetic  1.29 us (2%)
    pallas_call x1, Pallas kernels, run(): pl.pallas_call(functools.partial(kernel, groups), out_shape=jax.ShapeDtyp...  58.6 us
    reduce_sum x1, other arithmetic, per_device(): tokens = jnp.sum(lengths)  1.29 us

profile of v2, /device:TPU:1, one launch (start us, length us, event | category | flops | bytes accessed | tf_op | source)
XLA Modules:
  0.0 62.6 jit_solution(6427457041348090792)
XLA Ops:
  0.6 1.3 %reduce_sum.9 = s32[]{:T(128)} reduce(s32[16]{0:T(128)} %param.14, s32[]{:T(128)} %constant.0.clone.1), dimensions={0}, to_apply=%region_0.0 | reduce | flops 15 | bytes 72 | tf_op jit(solution)/shard_map/reduce_sum | solution.py:590
  3.2 58.8 %conditional.1 = (f32[8,128]{1,0:T(8,128)S(1)}) conditional(s32[]{:T(128)} %clamp.3, (bf16[64,512]{1,0:T(8,128)(2,1)}, f32[64,128]{1,0:T(8,128)}, s32[16]{0:T(128)}, s32[1,1024]{1,0:T(1,128)}, bf16[1024,512]{1,0:T(8,128)(2,1)}, /*index=5*/bf16[32,8,32,512]{3,2,1,0:T(8,128)(2,1)}) %tuple.29, (bf16[64,512]{1,0:T(8,128)(2,1)}, ...), branch_computations={%region_1.0_spmd, %region_2.0_spmd, %region_3.0_spmd} | conditional | bytes 8 | solution.py:592
  3.2 58.6 %gathered_head_512.1 = f32[8,128]{1,0:T(8,128)S(1)} custom-call(bf16[64,512]{1,0:T(8,128)(2,1)} %get-tuple-element.28.hidden, f32[64,128]{1,0:T(8,128)} %get-tuple-element.29.gain, s32[16]{0:T(128)} %get-tuple-element.42.lens, s32[1,1024]{1,0:T(1,128)} %get-tuple-element.43.ids, bf16[1024,512]{1,0:T(8,128)(2,1)} %get-tuple-element.44.student, ...), custom_call_target="tpu_custom_call" | custom-call | tf_op jit(solution)/shard_map/cond/branch_0_fun/gathered_head_512/pallas_call | solution.py:545
  62.1 0.5 slice_bitcast_fusion
